TPU v7x, 32 devices: a whole 2x2x4 slice. The times are simulated.
32 devices in a mesh: row: 8 (over y, x, core), col: 4 (over z).
Axes of the slice: x: 2, y: 2, z: 4, core: 2. Of those that a mesh axis runs over, the one named last changes fastest.
Arguments:
- queries: bfloat16 [128, 16, 1024], P('row', None, 'col'), may hold values from -30 to 30
- new_keys: bfloat16 [128, 1024], P('row', 'col'), may hold values from -6 to 6
- new_values: bfloat16 [128, 1024], P('row', 'col'), may hold values from -12 to 12
- cache_keys: bfloat16 [128, 128, 1024], P('row', None, 'col'), may hold values from -8 to 8
- cache_values: bfloat16 [128, 128, 1024], P('row', None, 'col'), may hold values from -12 to 12
- lengths: int32 [128], P('row'), may hold values from 64 to 128
- parents: int32 [128], P('row'), may hold values from 0 to 127, as said below
- residual: bfloat16 [128, 16, 1024], P('row', None, 'col'), may hold values from -20 to 20
- norm_gain: bfloat16 [16, 1024], P(None, 'col'), may hold values from 0.5 to 1.5
- vocab_weight: bfloat16 [16, 1024, 64128], P(None, 'col', 'row')
Outputs:
- logprobs: float32 [128, 64128], P('col', 'row')
Inputs may be any that keep to these rules, and one draw needn't show every extreme that they name: Among the 16 child beams of one index of row, at most 4 have their parents on the beams of any single index of row, and exactly 4 do for some index.
All inputs are finite; a program needn't handle non-finite values.
Results may differ from a plain program's by a relative error of at most 0.0015.
Values may be sent and summed in bfloat16 or wider, within the bound.
A program may use at most 128 MiB of HBM per device.

v0:
```python
import jax
import jax.numpy as jnp
from jax import lax
from jax.sharding import PartitionSpec as P

HEAD_DIM = 128
D = 16384


def from_partner(value, axis, distance):
    mask = 2**distance
    pairs = [(source, source ^ mask) for source in range(lax.axis_size(axis))]
    return lax.ppermute(value, axis, pairs)


def count_before(sources):
    entries = sources.shape[-1]
    earlier = jnp.arange(entries)[:, None] > jnp.arange(entries)[None, :]
    matching = sources[..., :, None] == sources[..., None, :]
    return jnp.sum(matching & earlier, axis=-1)


def attend(queries_in, key_cache, value_cache, key_new, value_new, live_rows):
    leading = queries_in.shape[:-2]
    group_size = queries_in.shape[-2]
    panel_width = queries_in.shape[-1]
    head_part = min(panel_width, HEAD_DIM)
    heads_here = panel_width // head_part
    context = key_cache.shape[-2]
    query_heads = queries_in.reshape(leading + (group_size, heads_here, head_part))
    key_heads = key_cache.reshape(leading + (context, heads_here, head_part))
    value_heads = value_cache.reshape(leading + (context, heads_here, head_part))
    fresh_key = key_new.reshape(leading + (heads_here, head_part))
    fresh_value = value_new.reshape(leading + (1, heads_here, head_part)).astype(jnp.float32)
    cached = jnp.einsum(
        "...jhe,...the->...jht", query_heads, key_heads, preferred_element_type=jnp.float32
    )
    own_score = jnp.einsum(
        "...jhe,...he->...jh", query_heads, fresh_key, preferred_element_type=jnp.float32
    )
    partners = (HEAD_DIM // head_part).bit_length() - 1
    for bit_index in range(partners):
        other_cached, other_own = from_partner((cached, own_score), "col", bit_index)
        cached = cached + other_cached
        own_score = own_score + other_own
    scale_factor = HEAD_DIM ** (-0.5)
    cached = cached * scale_factor
    own_score = own_score * scale_factor
    positions = lax.broadcasted_iota(jnp.int32, cached.shape, cached.ndim - 1)
    visible = positions < live_rows.reshape(leading + (1, 1, 1))
    peak_score = jnp.maximum(jnp.max(jnp.where(visible, cached, -jnp.inf), axis=-1), own_score)
    weight = jnp.where(visible, jnp.exp(cached - peak_score[..., None]), jnp.float32(0.0))
    weight_own = jnp.exp(own_score - peak_score)
    weight_sum = jnp.sum(weight, axis=-1) + weight_own
    rounded = weight.astype(jnp.bfloat16)
    rounded_own = lax.optimization_barrier(weight_own.astype(jnp.bfloat16)).astype(jnp.float32)
    summed = jnp.einsum(
        "...jht,...the->...jhe", rounded, value_heads, preferred_element_type=jnp.float32
    )
    own_part = rounded_own[..., None] * fresh_value
    result = (summed + own_part) / weight_sum[..., None]
    return result.reshape(leading + (group_size, panel_width)).astype(jnp.bfloat16)


def body(
    queries,
    new_keys,
    new_values,
    cache_keys,
    cache_values,
    lengths,
    parents,
    residual,
    norm_gain,
    vocab_weight,
):
    row_count = lax.axis_size("row")
    beam_count = parents.shape[0]
    slot_cap = max(2, (2 * beam_count + row_count - 1) // row_count)
    my_row = lax.axis_index("row")
    group_size = queries.shape[1]
    panel_width = queries.shape[2]
    source = parents // beam_count
    rank_in = count_before(source)
    slot_index = source * slot_cap + rank_in
    slot_range = jnp.arange(slot_cap, dtype=jnp.int32)
    all_parents, all_lengths = (
        lax.all_gather(parents, "row", axis=0, tiled=True),
        lax.all_gather(lengths, "row", axis=0, tiled=True),
    )
    parent_table = all_parents.reshape(row_count, beam_count)
    sources_all = parent_table // beam_count
    offsets_all = parent_table % beam_count
    ranks_all = count_before(sources_all)
    chosen = (sources_all[:, None, :] == my_row) & (
        ranks_all[:, None, :] == slot_range[None, :, None]
    )
    rows_sent = jnp.sum(jnp.where(chosen, offsets_all[:, None, :], 0), axis=2)
    got_keys, got_values = (
        lax.all_to_all(cache_keys[rows_sent], "row", split_axis=0, concat_axis=0, tiled=True),
        lax.all_to_all(cache_values[rows_sent], "row", split_axis=0, concat_axis=0, tiled=True),
    )
    context = cache_keys.shape[1]
    kept_keys = got_keys.reshape(row_count * slot_cap, context, panel_width)[slot_index]
    kept_values = got_values.reshape(row_count * slot_cap, context, panel_width)[slot_index]
    attended = attend(queries, kept_keys, kept_values, new_keys, new_values, all_lengths[parents])
    stream = residual.astype(jnp.float32) + attended.astype(jnp.float32)
    square_sums = lax.psum(jnp.sum(stream * stream, axis=(1, 2)), "col")
    scaling = lax.rsqrt(square_sums / D + 1e-05)
    normed = (stream * norm_gain.astype(jnp.float32)[None] * scaling[:, None, None]).astype(
        jnp.bfloat16
    )
    gathered = lax.all_gather(normed, "row", axis=0, tiled=True)
    flat_rows = gathered.reshape(gathered.shape[0], group_size * panel_width)
    flat_weight = vocab_weight.reshape(group_size * panel_width, vocab_weight.shape[2])
    logits = lax.psum_scatter(
        jnp.dot(flat_rows, flat_weight, preferred_element_type=jnp.float32),
        "col",
        scatter_dimension=0,
        tiled=True,
    )
    totals = lax.psum(jnp.sum(jnp.exp(logits), axis=1), "row")
    return logits - jnp.log(totals)[:, None]


def solution(mesh):
    placed = (
        P("row", None, "col"),
        P("row", "col"),
        P("row", "col"),
        P("row", None, "col"),
        P("row", None, "col"),
        P("row"),
        P("row"),
        P("row", None, "col"),
        P(None, "col"),
        P(None, "col", "row"),
    )
    return jax.shard_map(
        body, mesh=mesh, in_specs=placed, out_specs=P("col", "row"), check_vma=False
    )
```

profile of v0, /device:TPU:0, one launch (start us, length us, event | category | flops | bytes accessed | tf_op | source)
XLA Modules:
  0.0 248.6 jit_solution(12136826751953084435)
XLA Ops:
  6.5 1.3 dynamic-slice
  8.5 0.9 dynamic-update-slice
  9.4 0.8 dynamic-update-slice.1
  10.2 9.5 %all-reduce.2 = (s32[128]{0:T(128)S(1)}, s32[128]{0:T(128)S(1)}) all-reduce(s32[128]{0:T(128)S(1)} %dynamic-update-slice, s32[128]{0:T(128)S(1)} %dynamic-update-slice.1), channel_id=1, replica_groups=mesh['row'=8,'col'=4] {'row'}, use_global_device_ids=true, to_apply=%add | all-reduce | flops 256 | bytes 2048
  20.4 2.0 gather_fusion.3
  22.4 3.7 %all-to-all-start.1 = ((bf16[8,4,128,256]{3,2,1,0:T(8,128)(2,1)}), bf16[8,4,128,256]{3,2,1,0:T(8,128)(2,1)S(1)}, u32[]{:S(2)}, u32[]{:S(2)}) async-start(bf16[8,4,128,256]{3,2,1,0:T(8,128)(2,1)} %bitcast.5), calls=%async_computation.1 | async-start | bytes 4194304 | tf_op jit(solution)/shard_map/all_to_all | solution.py:100
  26.2 0.6 reshape.168
  26.8 0.6 convert_element_type.56
  27.4 2.0 gather_fusion
  29.5 23.3 %all-to-all-done.1 = bf16[8,4,128,256]{3,2,1,0:T(8,128)(2,1)S(1)} async-done(((bf16[8,4,128,256]{3,2,1,0:T(8,128)(2,1)}), bf16[8,4,128,256]{3,2,1,0:T(8,128)(2,1)S(1)}, u32[]{:S(2)}, u32[]{:S(2)}) %all-to-all-start.1) | async-done | bytes 2097184 | tf_op jit(solution)/shard_map/all_to_all | solution.py:100
  52.8 1.3 copy-done.2
  54.0 3.6 %all-to-all-start = ((bf16[8,4,128,256]{3,2,1,0:T(8,128)(2,1)}), bf16[8,4,128,256]{3,2,1,0:T(8,128)(2,1)S(1)}, u32[]{:S(2)}, u32[]{:S(2)}) async-start(bf16[8,4,128,256]{3,2,1,0:T(8,128)(2,1)} %bitcast.2), calls=%async_computation | async-start | bytes 4194304 | tf_op jit(solution)/shard_map/all_to_all | solution.py:101
  57.7 0.7 gather_fusion.2
  58.6 0.8 fusion.8
  59.4 2.2 gather_fusion.4
  61.6 1.3 copy.33
  63.0 1.7 select_reduce_fusion
  64.7 0.7 bitcast_maximum_fusion
  65.4 0.3 fusion.5
  65.7 0.7 fusion.22
  66.5 17.8 %all-to-all-done = bf16[8,4,128,256]{3,2,1,0:T(8,128)(2,1)S(1)} async-done(((bf16[8,4,128,256]{3,2,1,0:T(8,128)(2,1)}), bf16[8,4,128,256]{3,2,1,0:T(8,128)(2,1)S(1)}, u32[]{:S(2)}, u32[]{:S(2)}) %all-to-all-start) | async-done | bytes 2097184 | tf_op jit(solution)/shard_map/all_to_all | solution.py:101
  84.2 0.6 gather_fusion.1
  84.9 0.7 copy.32
  85.6 0.7 fusion.4
  86.8 12.0 %psum.14 = f32[16]{0:T(128)S(1)} all-reduce(f32[16]{0:T(128)S(1)} %multiply_reduce_fusion), channel_id=1, replica_groups=mesh['row'=8,'col'=4] {'col'}, use_global_device_ids=true, to_apply=%region_6.7 | all-reduce | flops 16 | bytes 128 | tf_op jit(solution)/shard_map/psum | solution.py:108
  98.8 0.7 multiply_convert_fusion
  99.6 20.0 %all-gather.2.cloned.1.call-done = bf16[128,16,256]{2,0,1:T(8,128)(2,1)} async-done(((bf16[16,16,256]{2,0,1:T(8,128)(2,1)}), bf16[128,16,256]{2,0,1:T(8,128)(2,1)}) %all-gather.2.cloned.1.call-update) | async-done | bytes 1048592 | tf_op jit(solution)/shard_map/all_gather | solution.py:113
  119.6 28.8 %convolution_bitcast_fusion = f32[128,8016]{1,0:T(8,128)} fusion(bf16[128,16,256]{2,0,1:T(8,128)(2,1)} %all-gather.2.cloned.1.call-done, bf16[16,256,8016]{1,2,0:T(8,128)(2,1)} %param.19), kind=kOutput, calls=%fused_computation.5 | convolution fusion | flops 8405385216 | bytes 70819840 | tf_op jit(solution)/shard_map/dot_general | solution.py:117
  148.5 75.9 %reduce-scatter.2.cloned.1.call-done = f32[32,8016]{1,0:T(8,128)} async-done(((f32[128,8016]{1,0:T(8,128)}), f32[32,8016]{1,0:T(8,128)}) %reduce-scatter.2.cloned.1.call-update) | async-done | bytes 1026064 | tf_op jit(solution)/shard_map/reduce_scatter | solution.py:116
  224.4 1.5 exponential_reduce_fusion
  225.8 13.6 %psum.15 = f32[32]{0:T(128)S(1)} all-reduce(f32[32]{0:T(128)S(1)} %exponential_reduce_fusion), channel_id=1, replica_groups=mesh['row'=8,'col'=4] {'row'}, use_global_device_ids=true, to_apply=%region_9.10 | all-reduce | flops 32 | bytes 256 | tf_op jit(solution)/shard_map/psum | solution.py:122
  239.5 2.3 broadcast_subtract_fusion
  (51 shorter events, 1.7 us)
Async XLA Ops:
  6.5 13.9 %copy-start = (bf16[16,128,256]{2,1,0:T(8,128)(2,1)S(1)}, bf16[16,128,256]{2,1,0:T(8,128)(2,1)}, u32[]{:S(2)}) copy-start(bf16[16,128,256]{2,1,0:T(8,128)(2,1)} %param.13) | copy-start | bytes 3145732
  22.4 3.8 %copy-start.8 = (bf16[16,256]{1,0:T(8,128)(2,1)S(1)}, bf16[16,256]{1,0:T(8,128)(2,1)}, u32[]{:S(2)}) copy-start(bf16[16,256]{1,0:T(8,128)(2,1)} %param.11) | copy-start | bytes 24580
  22.4 3.8 %copy-start.9 = (bf16[16,256]{1,0:T(8,128)(2,1)S(1)}, bf16[16,256]{1,0:T(8,128)(2,1)}, u32[]{:S(2)}) copy-start(bf16[16,256]{1,0:T(8,128)(2,1)} %param.12) | copy-start | bytes 24580
  22.4 4.4 %copy-start.10 = (bf16[16,256]{1,0:T(8,128)(2,1)S(1)}, bf16[16,256]{1,0:T(8,128)(2,1)}, u32[]{:S(2)}) copy-start(bf16[16,256]{1,0:T(8,128)(2,1)} %param.18) | copy-start | bytes 24580
  22.4 5.0 %copy-start.3 = (bf16[16,128,256]{2,1,0:T(8,128)(2,1)S(1)}, bf16[16,128,256]{2,1,0:T(8,128)(2,1)}, u32[]{:S(2)}) copy-start(bf16[16,128,256]{2,1,0:T(8,128)(2,1)} %param.14) | copy-start | bytes 3145732
  22.4 30.3 %all-to-all-start.1 = ((bf16[8,4,128,256]{3,2,1,0:T(8,128)(2,1)}), bf16[8,4,128,256]{3,2,1,0:T(8,128)(2,1)S(1)}, u32[]{:S(2)}, u32[]{:S(2)}) async-start(bf16[8,4,128,256]{3,2,1,0:T(8,128)(2,1)} %bitcast.5), calls=%async_computation.1 | async-start | bytes 4194304 | tf_op jit(solution)/shard_map/all_to_all | solution.py:100
  52.8 1.3 copy-start.2
  52.8 5.0 %copy-start.11 = (s32[16]{0:T(128)S(1)}, s32[16]{0:T(128)}, u32[]{:S(2)}) copy-start(s32[16]{0:T(128)} %param.16) | copy-start | bytes 196
  52.8 5.9 %copy-start.5 = (bf16[16,16,256]{2,1,0:T(8,128)(2,1)S(1)}, bf16[16,16,256]{2,1,0:T(8,128)(2,1)}, u32[]{:S(2)}) copy-start(bf16[16,16,256]{2,1,0:T(8,128)(2,1)} %param.10) | copy-start | bytes 393220
  54.0 30.2 %all-to-all-start = ((bf16[8,4,128,256]{3,2,1,0:T(8,128)(2,1)}), bf16[8,4,128,256]{3,2,1,0:T(8,128)(2,1)S(1)}, u32[]{:S(2)}, u32[]{:S(2)}) async-start(bf16[8,4,128,256]{3,2,1,0:T(8,128)(2,1)} %bitcast.2), calls=%async_computation | async-start | bytes 4194304 | tf_op jit(solution)/shard_map/all_to_all | solution.py:101
  57.7 62.0 %all-gather.2.cloned.1.call-start = ((), (), s32[]{:S(2)}) async-start(), calls=%async_computation.3 | async-start | bytes 1179648 | tf_op jit(solution)/shard_map/all_gather | solution.py:113
  84.2 1.3 copy-start.7
  85.5 1.1 copy-start.4
  85.6 13.2 %copy-start.6 = (f32[16,256]{1,0:T(8,128)S(1)}, f32[16,256]{1,0:T(8,128)}, u32[]{:S(2)}) copy-start(f32[16,256]{1,0:T(8,128)} %convert_element_type.56) | copy-start | bytes 49156
  99.6 124.8 %reduce-scatter.2.cloned.1.call-start = ((), (), s32[]{:S(2)}) async-start(), calls=%async_computation.4 | async-start | bytes 5160960 | tf_op jit(solution)/shard_map/reduce_scatter | solution.py:116
  148.5 93.3 %copy-start.1 = (bf16[16,128,256]{2,1,0:T(8,128)(2,1)S(1)}, bf16[16,128,256]{2,1,0:T(8,128)(2,1)}, u32[]{:S(2)}) copy-start(bf16[16,128,256]{2,1,0:T(8,128)(2,1)} %param.13) | copy-start | bytes 3145732
Sparse Core Ops, SparseCore 0:
  99.7 19.9 all-gather.1
  148.6 75.7 reduce-scatter.1
where the time goes:
time: 249 us
  waiting for transfers between devices  137 us (55%)
  blocking collectives  35 us (14%)
  matrix products  32 us (13%)
  local copies, waits for them, and re-layouts  15.1 us (6%)
  between operations  14.3 us (6%)
  other arithmetic  7.8 us (3%)
  starting transfers between devices  7.43 us (3%)
    reduce_scatter x1, waiting for transfers between devices, body(): lax.psum_scatter(jnp.dot(flat_rows, flat_weight, preferred_element_type=j...  75.9 us
    dot_general x1, matrix products, body(): jnp.dot(flat_rows, flat_weight, preferred_element_type=jnp.float32)  28.8 us
    all_to_all x1, waiting for transfers between devices, body(): lax.all_to_all(cache_keys[rows_sent], 'row', split_axis=0, concat_axis=0,...  23.3 us
    all_gather x1, waiting for transfers between devices, body(): gathered = lax.all_gather(normed, 'row', axis=0, tiled=True)  20 us
    all_to_all x1, waiting for transfers between devices, body(): lax.all_to_all(cache_values[rows_sent], 'row', split_axis=0, concat_axis=...  17.8 us
    psum x1, blocking collectives, body(): totals = lax.psum(jnp.sum(jnp.exp(logits), axis=1), 'row')  13.6 us
    psum x1, blocking collectives, body(): square_sums = lax.psum(jnp.sum(stream * stream, axis=(1, 2)), 'col')  12 us
    unnamed x1, blocking collectives  9.46 us
  transfers between devices with their start and end apart: 4, of which 4 were waited for; matrix products, arithmetic and copies ran while one was open for 5% of the time, Pallas kernels for 0%

commit v1 on v0

--- a/solution.py
+++ b/solution.py
@@ -77,33 +77,29 @@
     row_count = lax.axis_size("row")
     beam_count = parents.shape[0]
     slot_cap = max(2, (2 * beam_count + row_count - 1) // row_count)
-    my_row = lax.axis_index("row")
     group_size = queries.shape[1]
     panel_width = queries.shape[2]
     source = parents // beam_count
-    rank_in = count_before(source)
-    slot_index = source * slot_cap + rank_in
-    slot_range = jnp.arange(slot_cap, dtype=jnp.int32)
-    all_parents, all_lengths = (
-        lax.all_gather(parents, "row", axis=0, tiled=True),
-        lax.all_gather(lengths, "row", axis=0, tiled=True),
+    slot_index = source * slot_cap + count_before(source)
+    slots = row_count * slot_cap
+    taken = slot_index[None, :] == jnp.arange(slots, dtype=jnp.int32)[:, None]
+    child_of = jnp.sum(jnp.where(taken, jnp.arange(beam_count, dtype=jnp.int32)[None], 0), axis=1)
+    offset = (parents % beam_count).astype(jnp.bfloat16)
+    offset_row = jnp.broadcast_to(offset[:, None, None], (beam_count, 1, panel_width))
+    request = jnp.concatenate(
+        [queries, new_keys[:, None], new_values[:, None], offset_row], axis=1
+    )[child_of]
+    asked = lax.all_to_all(request, "row", split_axis=0, concat_axis=0, tiled=True)
+    wanted = asked[:, group_size + 2, 0].astype(jnp.int32)
+    answer = attend(
+        asked[:, :group_size],
+        cache_keys[wanted],
+        cache_values[wanted],
+        asked[:, group_size],
+        asked[:, group_size + 1],
+        lengths[wanted],
     )
-    parent_table = all_parents.reshape(row_count, beam_count)
-    sources_all = parent_table // beam_count
-    offsets_all = parent_table % beam_count
-    ranks_all = count_before(sources_all)
-    chosen = (sources_all[:, None, :] == my_row) & (
-        ranks_all[:, None, :] == slot_range[None, :, None]
-    )
-    rows_sent = jnp.sum(jnp.where(chosen, offsets_all[:, None, :], 0), axis=2)
-    got_keys, got_values = (
-        lax.all_to_all(cache_keys[rows_sent], "row", split_axis=0, concat_axis=0, tiled=True),
-        lax.all_to_all(cache_values[rows_sent], "row", split_axis=0, concat_axis=0, tiled=True),
-    )
-    context = cache_keys.shape[1]
-    kept_keys = got_keys.reshape(row_count * slot_cap, context, panel_width)[slot_index]
-    kept_values = got_values.reshape(row_count * slot_cap, context, panel_width)[slot_index]
-    attended = attend(queries, kept_keys, kept_values, new_keys, new_values, all_lengths[parents])
+    attended = lax.all_to_all(answer, "row", split_axis=0, concat_axis=0, tiled=True)[slot_index]
     stream = residual.astype(jnp.float32) + attended.astype(jnp.float32)
     square_sums = lax.psum(jnp.sum(stream * stream, axis=(1, 2)), "col")
     scaling = lax.rsqrt(square_sums / D + 1e-05)
@@ -113,12 +109,10 @@
     gathered = lax.all_gather(normed, "row", axis=0, tiled=True)
     flat_rows = gathered.reshape(gathered.shape[0], group_size * panel_width)
     flat_weight = vocab_weight.reshape(group_size * panel_width, vocab_weight.shape[2])
+    partial = jnp.dot(flat_rows, flat_weight, preferred_element_type=jnp.float32)
     logits = lax.psum_scatter(
-        jnp.dot(flat_rows, flat_weight, preferred_element_type=jnp.float32),
-        "col",
-        scatter_dimension=0,
-        tiled=True,
-    )
+        partial.astype(jnp.bfloat16), "col", scatter_dimension=0, tiled=True
+    ).astype(jnp.float32)
     totals = lax.psum(jnp.sum(jnp.exp(logits), axis=1), "row")
     return logits - jnp.log(totals)[:, None]
 

time: 249 us -> 173 us (0.69)
  waiting for transfers between devices: 137 us -> 70.1 us
  local copies, waits for them, and re-layouts: 15.1 us -> 5.48 us
  starting transfers between devices: 7.43 us -> 3.5 us
  blocking collectives: 35 us -> 38.7 us
    all_to_all x2 -> x1, waiting for transfers between devices: 41 us -> 6.78 us  [body(): lax.all_to_all(answer, 'row', split_axis=0, concat_axis=0, tiled=True)]
    reduce_scatter x1, waiting for transfers between devices: 75.9 us -> 43.3 us  [body(): lax.psum_scatter(partial.astype(jnp.bfloat16), 'col', scatter_dimension=0...]
    all_to_all x0 -> x1, blocking collectives: none -> 13.3 us  [body(): lax.all_to_all(request, 'row', split_axis=0, concat_axis=0, tiled=True)]
    unnamed x1 -> x0, blocking collectives: 9.46 us -> none
    gather x7 -> x5, local copies, waits for them, and re-layouts: 9.47 us -> 3.2 us  [the longest x1 0.7 us: body(): lengths[wanted]]
    unnamed x29 -> x16, local copies, waits for them, and re-layouts: 4.36 us -> 0.04 us
    all_to_all x2 -> x1, starting transfers between devices: 7.35 us -> 3.41 us  [body(): lax.all_to_all(answer, 'row', split_axis=0, concat_axis=0, tiled=True)]
  transfers between devices with their start and end apart: 4 -> 3, of which waited for: 4 -> 3; matrix products, arithmetic and copies ran while one was open for 5% -> 0% of each run, Pallas kernels for 0% -> 0%
where the time goes in v1:
time: 173 us; the launch traced here: 172 us
  waiting for transfers between devices  70.1 us (41%)
  blocking collectives  38.7 us (22%)
  matrix products  32 us (18%)
  between operations  13.6 us (8%)
  other arithmetic  8.92 us (5%)
  local copies, waits for them, and re-layouts  5.48 us (3%)
  starting transfers between devices  3.5 us (2%)
    reduce_scatter x1, waiting for transfers between devices, body(): lax.psum_scatter(partial.astype(jnp.bfloat16), 'col', scatter_dimension=0...  43.3 us
    dot_general x1, matrix products, body(): jnp.dot(flat_rows, flat_weight, preferred_element_type=jnp.float32)  28.6 us
    all_gather x1, waiting for transfers between devices, body(): gathered = lax.all_gather(normed, 'row', axis=0, tiled=True)  20 us
    psum x1, blocking collectives, body(): totals = lax.psum(jnp.sum(jnp.exp(logits), axis=1), 'row')  13.4 us
    all_to_all x1, blocking collectives, body(): lax.all_to_all(request, 'row', split_axis=0, concat_axis=0, tiled=True)  13.3 us
    psum x1, blocking collectives, body(): square_sums = lax.psum(jnp.sum(stream * stream, axis=(1, 2)), 'col')  12 us
    all_to_all x1, waiting for transfers between devices, body(): lax.all_to_all(answer, 'row', split_axis=0, concat_axis=0, tiled=True)  6.78 us
  transfers between devices with their start and end apart: 3, of which 3 were waited for; matrix products, arithmetic and copies ran while one was open for 0% of the time, Pallas kernels for 0%

profile of v1, /device:TPU:0, one launch (start us, length us, event | category | flops | bytes accessed | tf_op | source)
XLA Modules:
  0.0 172.3 jit_solution(5072314166568350100)
XLA Ops:
  6.5 0.8 and_select_fusion
  7.3 0.7 copy.26
  8.0 0.7 copy.25
  8.7 0.2 convert_reduce_fusion
  8.9 0.1 select_reduce_fusion.1
  9.0 0.1 broadcast_in_dim.30
  9.1 1.0 pad_maximum_fusion
  10.1 0.6 gather_fusion
  10.7 13.3 %all_to_all.10 = bf16[32,19,256]{2,1,0:T(8,128)(2,1)S(1)} all-to-all(bf16[32,19,256]{2,1,0:T(8,128)(2,1)S(1)} %gather_fusion), channel_id=1, replica_groups=mesh['row'=8,'col'=4] {'row'}, dimensions={0} | all-to-all | bytes 622592 | tf_op jit(solution)/shard_map/all_to_all | solution.py:92
  24.0 0.7 fusion.41
  24.7 0.7 gather_fusion.2
  25.4 0.7 gather_fusion.3
  26.1 0.2 fusion.32
  26.3 1.3 select_reduce_fusion
  27.7 0.5 fusion.29
  28.2 0.7 fusion.48
  28.8 0.6 convert_element_type.70
  29.4 0.7 gather_fusion.1
  30.2 1.8 %fusion.25 = bf16[32,2,2,8,128]{4,3,2,1,0:T(8,128)(2,1)S(1)} fusion(f32[32,16,2,128]{3,1,2,0:T(8,128)} %copy-done.4, f32[32,16,2]{1,2,0:T(2,128)} %get-tuple-element.8, f32[32,2,128]{2,1,0:T(2,128)S(1)} %bitcast.97, f32[32,16,2]{1,2,0:T(2,128)} %convert_element_type.70, f32[32,16,2]{1,2,0:T(2,128)} %copy-done.6, s32[32]{0:T(128)S(1)} %gather_fusion.2, ...), kind=kOutput, calls=%fused_computation.21 | convolution fusion | flops 34603008 | bytes 2928768 | tf_op jit(solution)/shard_map/...jht,...the->...jhe/dot_general | solution.py:57
  32.0 0.7 copy.77
  32.8 3.4 %all-to-all-start.1 = ((bf16[32,16,256]{2,1,0:T(8,128)(2,1)}), bf16[32,16,256]{2,1,0:T(8,128)(2,1)S(1)}, u32[]{:S(2)}, u32[]{:S(2)}) async-start(bf16[32,16,256]{2,1,0:T(8,128)(2,1)} %bitcast.94), calls=%async_computation.1 | async-start | bytes 524288 | tf_op jit(solution)/shard_map/all_to_all | solution.py:102
  36.3 6.8 %all-to-all-done.1 = bf16[32,16,256]{2,1,0:T(8,128)(2,1)S(1)} async-done(((bf16[32,16,256]{2,1,0:T(8,128)(2,1)}), bf16[32,16,256]{2,1,0:T(8,128)(2,1)S(1)}, u32[]{:S(2)}, u32[]{:S(2)}) %all-to-all-start.1) | async-done | bytes 262176 | tf_op jit(solution)/shard_map/all_to_all | solution.py:102
  43.1 0.6 gather_fusion.4
  43.6 0.2 multiply_reduce_fusion
  43.8 12.0 %psum.14 = f32[16]{0:T(128)S(1)} all-reduce(f32[16]{0:T(128)S(1)} %multiply_reduce_fusion), channel_id=1, replica_groups=mesh['row'=8,'col'=4] {'col'}, use_global_device_ids=true, to_apply=%region_5.6 | all-reduce | flops 16 | bytes 128 | tf_op jit(solution)/shard_map/psum | solution.py:104
  55.8 0.8 multiply_convert_fusion
  56.6 20.0 %all-gather.2.cloned.1.call-done = bf16[128,16,256]{2,0,1:T(8,128)(2,1)} async-done(((bf16[16,16,256]{2,0,1:T(8,128)(2,1)}), bf16[128,16,256]{2,0,1:T(8,128)(2,1)}) %all-gather.2.cloned.1.call-update) | async-done | bytes 1048592 | tf_op jit(solution)/shard_map/all_gather | solution.py:109
  76.6 28.6 %fusion = bf16[128,8016]{1,0:T(8,128)(2,1)} fusion(bf16[128,16,256]{2,0,1:T(8,128)(2,1)} %all-gather.2.cloned.1.call-done, bf16[16,256,8016]{1,2,0:T(8,128)(2,1)} %param.19), kind=kOutput, calls=%fused_computation.6 | convolution fusion | flops 8406411264 | bytes 68767744 | tf_op jit(solution)/shard_map/dot_general | solution.py:112
  105.3 43.3 %reduce-scatter.2.cloned.1.call-done = bf16[32,8016]{1,0:T(8,128)(2,1)} async-done(((bf16[128,8016]{1,0:T(8,128)(2,1)}), bf16[32,8016]{1,0:T(8,128)(2,1)}) %reduce-scatter.2.cloned.1.call-update) | async-done | bytes 513040 | tf_op jit(solution)/shard_map/reduce_scatter | solution.py:113
  148.6 1.3 fusion.28
  149.9 13.4 %psum.15 = f32[32]{0:T(128)S(1)} all-reduce(f32[32]{0:T(128)S(1)} %fusion.28), channel_id=1, replica_groups=mesh['row'=8,'col'=4] {'row'}, use_global_device_ids=true, to_apply=%region_8.9 | all-reduce | flops 32 | bytes 256 | tf_op jit(solution)/shard_map/psum | solution.py:116
  163.3 2.1 %convert_subtract_fusion = f32[32,8016]{1,0:T(8,128)} fusion(bf16[32,8016]{1,0:T(8,128)(2,1)} %reduce-scatter.2.cloned.1.call-done, f32[32]{0:T(128)S(1)} %log.3), kind=kLoop, calls=%fused_computation.13 | loop fusion | flops 513024 | bytes 1539200 | tf_op jit(solution)/shard_map/sub | solution.py:117
  (31 shorter events, 0.3 us)
Async XLA Ops:
  6.5 18.9 %copy-start = (bf16[16,128,256]{2,1,0:T(8,128)(2,1)S(1)}, bf16[16,128,256]{2,1,0:T(8,128)(2,1)}, u32[]{:S(2)}) copy-start(bf16[16,128,256]{2,1,0:T(8,128)(2,1)} %param.13) | copy-start | bytes 3145732
  6.5 18.1 %copy-start.2 = (s32[16]{0:T(128)S(1)}, s32[16]{0:T(128)}, u32[]{:S(2)}) copy-start(s32[16]{0:T(128)} %param.15) | copy-start | bytes 196
  26.3 3.1 %copy-start.3 = (bf16[16,128,256]{2,1,0:T(8,128)(2,1)S(1)}, bf16[16,128,256]{2,1,0:T(8,128)(2,1)}, u32[]{:S(2)}) copy-start(bf16[16,128,256]{2,1,0:T(8,128)(2,1)} %param.14) | copy-start | bytes 3145732
  27.6 1.2 copy-start.4
  27.7 1.1 copy-start.6
  30.2 6.1 %copy-start.7 = (bf16[16,256]{1,0:T(8,128)(2,1)S(1)}, bf16[16,256]{1,0:T(8,128)(2,1)}, u32[]{:S(2)}) copy-start(bf16[16,256]{1,0:T(8,128)(2,1)} %param.18) | copy-start | bytes 24580
  30.2 13.4 %copy-start.5 = (bf16[16,16,256]{2,1,0:T(8,128)(2,1)S(1)}, bf16[16,16,256]{2,1,0:T(8,128)(2,1)}, u32[]{:S(2)}) copy-start(bf16[16,16,256]{2,1,0:T(8,128)(2,1)} %param.17) | copy-start | bytes 393220
  32.8 10.3 %all-to-all-start.1 = ((bf16[32,16,256]{2,1,0:T(8,128)(2,1)}), bf16[32,16,256]{2,1,0:T(8,128)(2,1)S(1)}, u32[]{:S(2)}, u32[]{:S(2)}) async-start(bf16[32,16,256]{2,1,0:T(8,128)(2,1)} %bitcast.94), calls=%async_computation.1 | async-start | bytes 524288 | tf_op jit(solution)/shard_map/all_to_all | solution.py:102
  36.2 40.4 %all-gather.2.cloned.1.call-start = ((), (), s32[]{:S(2)}) async-start(), calls=%async_computation.3 | async-start | bytes 1179648 | tf_op jit(solution)/shard_map/all_gather | solution.py:109
  56.6 92.0 %reduce-scatter.2.cloned.1.call-start = ((), (), s32[]{:S(2)}) async-start(), calls=%async_computation.4 | async-start | bytes 2580480 | tf_op jit(solution)/shard_map/reduce_scatter | solution.py:113
  76.6 88.8 %copy-start.1 = (bf16[16,128,256]{2,1,0:T(8,128)(2,1)S(1)}, bf16[16,128,256]{2,1,0:T(8,128)(2,1)}, u32[]{:S(2)}) copy-start(bf16[16,128,256]{2,1,0:T(8,128)(2,1)} %param.13) | copy-start | bytes 3145732
Sparse Core Ops, SparseCore 0:
  56.7 19.8 all-gather.1
  105.4 43.1 reduce-scatter.1

commit v2 on v1

--- a/solution.py
+++ b/solution.py
@@ -1,10 +1,19 @@
+import functools
+
 import jax
 import jax.numpy as jnp
 from jax import lax
+from jax.experimental import pallas as pl
+from jax.experimental.pallas import tpu as pltpu
 from jax.sharding import PartitionSpec as P
 
 HEAD_DIM = 128
 D = 16384
+MESH = pl.DeviceIdType.MESH
+LANES = 128
+CHUNK = 512
+PIECE = 256
+SLOTS = 10
 
 
 def from_partner(value, axis, distance):
@@ -60,6 +69,338 @@
     own_part = rounded_own[..., None] * fresh_value
     result = (summed + own_part) / weight_sum[..., None]
     return result.reshape(leading + (group_size, panel_width)).astype(jnp.bfloat16)
+
+
+def project_kernel(
+    n_row,
+    n_col,
+    x_ref,
+    square_ref,
+    weight_ref,
+    out_ref,
+    rows,
+    squares,
+    squares_in,
+    weights,
+    weights_last,
+    own,
+    outgoing,
+    incoming,
+    total_out,
+    total_in,
+    weight_sem,
+    last_sem,
+    gather_send,
+    gather_recv,
+    gather_sq_send,
+    gather_sq_recv,
+    square_send,
+    square_recv,
+    part_send,
+    part_recv,
+    total_send,
+    total_recv,
+):
+    row, col = lax.axis_index("row"), lax.axis_index("col")
+    beams = x_ref.shape[0]
+    groups, vocab, panel = weight_ref.shape
+    owned = out_ref.shape[0]
+    full = vocab // CHUNK
+    last = vocab - full * CHUNK
+    last_pad = own.shape[1] - full * CHUNK
+    slots = weights.shape[0]
+    chips = n_row // 2
+    core = lax.rem(row, 2)
+    chip = lax.div(row, 2)
+
+    def fetch(chunk, slot):
+        return pltpu.make_async_copy(
+            weight_ref.at[:, pl.ds(pl.multiple_of(chunk * CHUNK, CHUNK), CHUNK), :],
+            weights.at[slot],
+            weight_sem.at[slot],
+        )
+
+    def fetch_last():
+        return pltpu.make_async_copy(
+            weight_ref.at[:, pl.ds(full * CHUNK, last), :], weights_last, last_sem.at[0]
+        )
+
+    if last:
+        fetch_last().start()
+    for slot in range(min(slots, full)):
+        fetch(slot, slot).start()
+
+    barrier = pltpu.get_barrier_semaphore()
+    for k in range(1, n_row):
+        pl.semaphore_signal(
+            barrier, inc=1, device_id=(lax.rem(row + k, n_row), col), device_id_type=MESH
+        )
+    for k in range(1, n_col):
+        pl.semaphore_signal(
+            barrier, inc=1, device_id=(row, lax.rem(col + k, n_col)), device_id_type=MESH
+        )
+    pl.semaphore_wait(barrier, n_row - 1 + n_col - 1)
+
+    def place(of_row):
+        first = of_row * beams
+        block = lax.rem(lax.div(first, owned) - col + n_col, n_col)
+        return pl.ds(pl.multiple_of(block * owned + lax.rem(first, owned), beams), beams)
+
+    def share(source, target, of_row, to_row, send, recv, index):
+        return pltpu.make_async_remote_copy(
+            src_ref=source,
+            dst_ref=target.at[place(of_row)],
+            send_sem=send.at[index],
+            recv_sem=recv.at[index],
+            device_id=(to_row, col),
+            device_id_type=MESH,
+        )
+
+    mate = chip * 2 + 1 - core
+    started = []
+    for k in list(range(1, chips)) + [0]:
+        to_row = lax.rem(chip + k, chips) * 2 + core if k else mate
+        one = share(x_ref, rows, row, to_row, gather_send, gather_recv, k)
+        two = share(square_ref, squares, row, to_row, gather_sq_send, gather_sq_recv, k)
+        one.start()
+        two.start()
+        started += [one, two]
+    rows[place(row)] = x_ref[...]
+    squares[place(row)] = square_ref[...]
+    pad = own.shape[1] - full * CHUNK
+    if pad > last:
+        edge = own.shape[1] - LANES
+        outgoing[:, :, edge:] = jnp.zeros(outgoing.shape[:2] + (LANES,), outgoing.dtype)
+        own[:, edge:] = jnp.zeros((owned, LANES), own.dtype)
+    forwarded = []
+    for k in range(1, chips):
+        from_row = lax.rem(chip - k + chips, chips) * 2 + core
+        share(rows.at[place(from_row)], rows, row, mate, gather_send, gather_recv, k).wait_recv()
+        share(
+            squares.at[place(from_row)], squares, row, mate, gather_sq_send, gather_sq_recv, k
+        ).wait_recv()
+        one = share(
+            rows.at[place(from_row)], rows, from_row, mate, gather_send, gather_recv, chips + k
+        )
+        two = share(
+            squares.at[place(from_row)],
+            squares,
+            from_row,
+            mate,
+            gather_sq_send,
+            gather_sq_recv,
+            chips + k,
+        )
+        one.start()
+        two.start()
+        forwarded += [one, two]
+    for copy in started[-2:]:
+        copy.wait_recv()
+    for copy in forwarded:
+        copy.wait_recv()
+
+    square_copies = []
+    for j in range(1, n_col):
+        copy = pltpu.make_async_remote_copy(
+            src_ref=squares.at[pl.ds(j * owned, owned)],
+            dst_ref=squares_in.at[j - 1],
+            send_sem=square_send.at[j - 1],
+            recv_sem=square_recv.at[j - 1],
+            device_id=(row, lax.rem(col + j, n_col)),
+            device_id_type=MESH,
+        )
+        copy.start()
+        square_copies.append(copy)
+
+    def part_copy(j, chunk, columns):
+        return pltpu.make_async_remote_copy(
+            src_ref=outgoing.at[j - 1, :, columns],
+            dst_ref=incoming.at[j - 1, :, columns],
+            send_sem=part_send.at[chunk, j - 1],
+            recv_sem=part_recv.at[chunk, j - 1],
+            device_id=(row, lax.rem(col + j, n_col)),
+            device_id_type=MESH,
+        )
+
+    def columns_of(chunk):
+        return pl.ds(pl.multiple_of(chunk * CHUNK, CHUNK), CHUNK)
+
+    last_columns = pl.ds(full * CHUNK, last_pad)
+
+    def product(block, first, width):
+        part = jnp.zeros((rows.shape[0], width), jnp.float32)
+        for group in range(groups):
+            part = part + lax.dot_general(
+                rows[:, group * panel : (group + 1) * panel],
+                block[group, first : first + width],
+                (((1,), (1,)), ((), ())),
+                preferred_element_type=jnp.float32,
+            )
+        return part
+
+    def keep(part, columns):
+        own[:, columns] = part[:owned]
+        for j in range(1, n_col):
+            outgoing[j - 1, :, columns] = part[j * owned : (j + 1) * owned].astype(jnp.bfloat16)
+
+    if last:
+        fetch_last().wait()
+        for first in range(0, last, PIECE):
+            width = min(PIECE, last - first)
+            keep(
+                product(weights_last, first, width),
+                slice(full * CHUNK + first, full * CHUNK + first + width),
+            )
+        for j in range(1, n_col):
+            part_copy(j, full, last_columns).start()
+
+    def multiply(chunk, carry):
+        slot = lax.rem(chunk, slots)
+        fetch(chunk, slot).wait()
+        for first in range(0, CHUNK, PIECE):
+            columns = pl.ds(pl.multiple_of(chunk * CHUNK + first, PIECE), PIECE)
+            keep(product(weights.at[slot], first, PIECE), columns)
+        for j in range(1, n_col):
+            part_copy(j, chunk, columns_of(chunk)).start()
+
+        @pl.when(chunk + slots < full)
+        def _():
+            fetch(chunk + slots, slot).start()
+
+        return carry
+
+    lax.fori_loop(0, full, multiply, 0)
+
+    square_sum = squares[:owned]
+    for j in range(1, n_col):
+        square_copies[j - 1].wait_recv()
+        square_sum = square_sum + squares_in[j - 1]
+    scale = lax.rsqrt(square_sum / D + 1e-05)[:, :1]
+
+    def combine(chunk, columns):
+        logits = own[:, columns]
+        for j in range(1, n_col):
+            part_copy(j, chunk, columns).wait_recv()
+            logits = logits + incoming[j - 1, :, columns].astype(jnp.float32)
+        logits = logits * scale
+        own[:, columns] = logits
+        return logits
+
+    sums = jnp.zeros((owned, 1), jnp.float32)
+    if last:
+        logits = combine(full, last_columns)
+        sums = sums + jnp.sum(jnp.exp(logits[:, :last]), axis=1, keepdims=True)
+
+    def finish(chunk, sums):
+        logits = combine(chunk, columns_of(chunk))
+        return sums + jnp.sum(jnp.exp(logits), axis=1, keepdims=True)
+
+    sums = lax.fori_loop(0, full, finish, sums)
+    total_out[...] = jnp.broadcast_to(sums, total_out.shape)
+    total_copies = []
+    for k in range(1, n_row):
+        copy = pltpu.make_async_remote_copy(
+            src_ref=total_out,
+            dst_ref=total_in.at[k - 1],
+            send_sem=total_send.at[k - 1],
+            recv_sem=total_recv.at[k - 1],
+            device_id=(lax.rem(row + k, n_row), col),
+            device_id_type=MESH,
+        )
+        copy.start()
+        total_copies.append(copy)
+    for copy in started + forwarded + square_copies:
+        copy.wait_send()
+
+    def sent(chunk, carry):
+        for j in range(1, n_col):
+            part_copy(j, chunk, columns_of(chunk)).wait_send()
+        return carry
+
+    lax.fori_loop(0, full, sent, 0)
+    if last:
+        for j in range(1, n_col):
+            part_copy(j, full, last_columns).wait_send()
+    total = total_out[...]
+    for copy in total_copies:
+        copy.wait_recv()
+    for k in range(1, n_row):
+        total = total + total_in[k - 1]
+    out_ref[...] = own[:, :vocab] - jnp.log(total)[:, :1]
+    for copy in total_copies:
+        copy.wait_send()
+
+
+def project(x, square_sums, weight):
+    n_row, n_col = lax.axis_size("row"), lax.axis_size("col")
+    beams, depth = x.shape
+    groups, vocab, panel = weight.shape
+    everyone = beams * n_row
+    owned = everyone // n_col
+    full = vocab // CHUNK
+    last = vocab - full * CHUNK
+    wide = full * CHUNK + -(-last // LANES) * LANES
+    slots = min(SLOTS, full)
+    chips = n_row // 2
+    others = n_col - 1
+    dma = pltpu.SemaphoreType.DMA
+    vmem = pl.BlockSpec(memory_space=pltpu.VMEM)
+    return pl.pallas_call(
+        functools.partial(project_kernel, n_row, n_col),
+        out_shape=jax.ShapeDtypeStruct((owned, vocab), jnp.float32),
+        in_specs=[vmem, vmem, pl.BlockSpec(memory_space=pl.ANY)],
+        out_specs=vmem,
+        scratch_shapes=[
+            pltpu.VMEM((everyone, depth), jnp.bfloat16),
+            pltpu.VMEM((everyone, LANES), jnp.float32),
+            pltpu.VMEM((others, owned, LANES), jnp.float32),
+            pltpu.VMEM((slots, groups, CHUNK, panel), jnp.bfloat16),
+            pltpu.VMEM((groups, max(last, 16), panel), jnp.bfloat16),
+            pltpu.VMEM((owned, wide), jnp.float32),
+            pltpu.VMEM((others, owned, wide), jnp.bfloat16),
+            pltpu.VMEM((others, owned, wide), jnp.bfloat16),
+            pltpu.VMEM((owned, LANES), jnp.float32),
+            pltpu.VMEM((n_row - 1, owned, LANES), jnp.float32),
+            dma((slots,)),
+            dma((1,)),
+            dma((2 * chips,)),
+            dma((2 * chips,)),
+            dma((2 * chips,)),
+            dma((2 * chips,)),
+            dma((others,)),
+            dma((others,)),
+            dma((full + 1, others)),
+            dma((full + 1, others)),
+            dma((n_row - 1,)),
+            dma((n_row - 1,)),
+        ],
+        compiler_params=pltpu.CompilerParams(
+            collective_id=0, has_side_effects=True, vmem_limit_bytes=56 * 2**20
+        ),
+        cost_estimate=pl.CostEstimate(
+            flops=2 * everyone * depth * vocab,
+            bytes_accessed=2 * depth * vocab,
+            transcendentals=owned * vocab,
+        ),
+    )(x, square_sums, weight)
+
+
+def project_whole(stream, norm_gain, vocab_weight):
+    group_size, panel_width = norm_gain.shape
+    square_sums = lax.psum(jnp.sum(stream * stream, axis=(1, 2)), "col")
+    scaling = lax.rsqrt(square_sums / D + 1e-05)
+    normed = (stream * norm_gain.astype(jnp.float32)[None] * scaling[:, None, None]).astype(
+        jnp.bfloat16
+    )
+    gathered = lax.all_gather(normed, "row", axis=0, tiled=True)
+    flat_rows = gathered.reshape(gathered.shape[0], group_size * panel_width)
+    flat_weight = vocab_weight.reshape(group_size * panel_width, vocab_weight.shape[2])
+    partial = jnp.dot(flat_rows, flat_weight, preferred_element_type=jnp.float32)
+    logits = lax.psum_scatter(
+        partial.astype(jnp.bfloat16), "col", scatter_dimension=0, tiled=True
+    ).astype(jnp.float32)
+    totals = lax.psum(jnp.sum(jnp.exp(logits), axis=1), "row")
+    return logits - jnp.log(totals)[:, None]
 
 
 def body(
@@ -101,20 +442,14 @@
     )
     attended = lax.all_to_all(answer, "row", split_axis=0, concat_axis=0, tiled=True)[slot_index]
     stream = residual.astype(jnp.float32) + attended.astype(jnp.float32)
-    square_sums = lax.psum(jnp.sum(stream * stream, axis=(1, 2)), "col")
-    scaling = lax.rsqrt(square_sums / D + 1e-05)
-    normed = (stream * norm_gain.astype(jnp.float32)[None] * scaling[:, None, None]).astype(
-        jnp.bfloat16
-    )
-    gathered = lax.all_gather(normed, "row", axis=0, tiled=True)
-    flat_rows = gathered.reshape(gathered.shape[0], group_size * panel_width)
-    flat_weight = vocab_weight.reshape(group_size * panel_width, vocab_weight.shape[2])
-    partial = jnp.dot(flat_rows, flat_weight, preferred_element_type=jnp.float32)
-    logits = lax.psum_scatter(
-        partial.astype(jnp.bfloat16), "col", scatter_dimension=0, tiled=True
-    ).astype(jnp.float32)
-    totals = lax.psum(jnp.sum(jnp.exp(logits), axis=1), "row")
-    return logits - jnp.log(totals)[:, None]
+    if panel_width % LANES or vocab_weight.shape[2] % 16:
+        return project_whole(stream, norm_gain, vocab_weight)
+    square_sums = jnp.broadcast_to(
+        jnp.sum(stream * stream, axis=(1, 2))[:, None], (beam_count, LANES)
+    )
+    gained = (stream * norm_gain.astype(jnp.float32)[None]).astype(jnp.bfloat16)
+    flat_rows = gained.reshape(beam_count, group_size * panel_width)
+    return project(flat_rows, square_sums, jnp.swapaxes(vocab_weight, 1, 2))
 
 
 def solution(mesh):

time: 173 us -> 109 us (0.63)
  Pallas kernels: 0 us -> 67.3 us
  waiting for transfers between devices: 70.1 us -> 6.83 us
  matrix products: 32 us -> 3.37 us
  blocking collectives: 38.7 us -> 13.3 us
  between operations: 13.6 us -> 0.18 us
  other arithmetic: 8.92 us -> 4.75 us
  local copies, waits for them, and re-layouts: 5.48 us -> 9.08 us
    pallas_call x0 -> x1, Pallas kernels: none -> 67.3 us  [project(): pl.pallas_call(functools.partial(project_kernel, n_row, n_col), out_shape...]
    reduce_scatter x1 -> x0, waiting for transfers between devices: 43.3 us -> none  [body(): lax.psum_scatter(partial.astype(jnp.bfloat16), 'col', scatter_dimension=0...]
    dot_general x1 -> x0, matrix products: 28.6 us -> none  [body(): jnp.dot(flat_rows, flat_weight, preferred_element_type=jnp.float32)]
    psum x2 -> x0, blocking collectives: 25.4 us -> none  [the longest x1 13.4 us: body(): totals = lax.psum(jnp.sum(jnp.exp(logits), axis=1), 'row')]
    all_gather x1 -> x0, waiting for transfers between devices: 20 us -> none  [body(): gathered = lax.all_gather(normed, 'row', axis=0, tiled=True)]
    unnamed x16 -> x18, local copies, waits for them, and re-layouts: 0.04 us -> 2.98 us
    sub x1 -> x0, other arithmetic: 2.14 us -> none  [body(): return logits - jnp.log(totals)[:, None]]
  transfers between devices with their start and end apart: 3 -> 1, of which waited for: 3 -> 1; matrix products, arithmetic and copies ran while one was open for 0% -> 0% of each run, Pallas kernels for 0% -> 0%
where the time goes in v2:
time: 109 us; the launch traced here: 108 us
  Pallas kernels  67.3 us (62%)
  blocking collectives  13.3 us (12%)
  local copies, waits for them, and re-layouts  9.08 us (8%)
  waiting for transfers between devices  6.83 us (6%)
  other arithmetic  4.75 us (4%)
  starting transfers between devices  3.41 us (3%)
  matrix products  3.37 us (3%)
    pallas_call x1, Pallas kernels, project(): pl.pallas_call(functools.partial(project_kernel, n_row, n_col), out_shape...  67.3 us
    all_to_all x1, blocking collectives, body(): lax.all_to_all(request, 'row', split_axis=0, concat_axis=0, tiled=True)  13.3 us
    all_to_all x1, waiting for transfers between devices, body(): lax.all_to_all(answer, 'row', split_axis=0, concat_axis=0, tiled=True)  6.83 us
    all_to_all x1, starting transfers between devices, body(): lax.all_to_all(answer, 'row', split_axis=0, concat_axis=0, tiled=True)  3.41 us
    unnamed x18, local copies, waits for them, and re-layouts  2.98 us
  transfers between devices with their start and end apart: 1, of which 1 were waited for; matrix products, arithmetic and copies ran while one was open for 0% of the time, Pallas kernels for 0%

profile of v2, /device:TPU:0, one launch (start us, length us, event | category | flops | bytes accessed | tf_op | source)
XLA Modules:
  0.0 108.3 jit_solution(9321475004471198288)
XLA Ops:
  0.0 0.8 and_select_fusion
  0.8 0.7 copy.22
  1.5 0.7 copy.21
  2.2 0.2 convert_reduce_fusion
  2.4 0.1 select_reduce_fusion.1
  2.5 0.1 broadcast_in_dim.32
  2.6 1.0 pad_maximum_fusion
  3.6 0.6 gather_fusion
  4.2 13.3 %all_to_all.10 = bf16[32,19,256]{2,1,0:T(8,128)(2,1)S(1)} all-to-all(bf16[32,19,256]{2,1,0:T(8,128)(2,1)S(1)} %gather_fusion), channel_id=1, replica_groups=mesh['row'=8,'col'=4] {'row'}, dimensions={0} | all-to-all | bytes 622592 | tf_op jit(solution)/shard_map/all_to_all | solution.py:433
  17.5 0.7 fusion.39
  18.2 0.7 gather_fusion.2
  18.9 0.7 gather_fusion.3
  19.6 0.2 fusion.30
  19.8 1.3 %select_reduce_fusion = (f32[32,16,2]{1,2,0:T(2,128)S(1)}, f32[32,16,2,128]{3,1,2,0:T(8,128)S(1)}) fusion(s32[32]{0:T(128)S(1)} %gather_fusion.2, bf16[32,128,256]{2,1,0:T(8,128)(2,1)S(1)} %gather_fusion.3, bf16[32,19,256]{2,1,0:T(8,128)(2,1)S(1)} %all_to_all.10), kind=kOutput, calls=%fused_computation.19 | convolution fusion | flops 34077696 | bytes 2888192 | tf_op jit(solution)/shard_map/...jhe,...the->...jht/dot_general | solution.py:44
  21.1 0.0 copy-start.6
  21.1 0.5 fusion.27
  21.6 0.7 fusion.46
  22.3 0.0 copy-done.4
  22.3 0.6 convert_element_type.64
  22.9 0.7 gather_fusion.1
  23.6 0.0 copy-start.7
  23.6 0.0 copy-start.5
  23.7 1.8 %fusion.24 = bf16[32,2,2,8,128]{4,3,2,1,0:T(8,128)(2,1)S(1)} fusion(f32[32,16,2,128]{3,1,2,0:T(8,128)} %copy-done.4, f32[32,16,2]{1,2,0:T(2,128)} %get-tuple-element.10, f32[32,2,128]{2,1,0:T(2,128)S(1)} %bitcast.97, f32[32,16,2]{1,2,0:T(2,128)} %convert_element_type.64, f32[32,16,2]{1,2,0:T(2,128)} %copy-done.6, s32[32]{0:T(128)S(1)} %gather_fusion.2, ...), kind=kOutput, calls=%fused_computation.17 | convolution fusion | flops 34603008 | bytes 2928768 | tf_op jit(solution)/shard_map/...jht,...the->...jhe/dot_general | solution.py:66
  25.5 0.7 copy.69
  26.2 3.4 %all-to-all-start.1 = ((bf16[32,16,256]{2,1,0:T(8,128)(2,1)}), bf16[32,16,256]{2,1,0:T(8,128)(2,1)S(1)}, u32[]{:S(2)}, u32[]{:S(2)}) async-start(bf16[32,16,256]{2,1,0:T(8,128)(2,1)} %bitcast.91), calls=%async_computation.1 | async-start | bytes 524288 | tf_op jit(solution)/shard_map/all_to_all | solution.py:443
  29.7 6.8 %all-to-all-done.1 = bf16[32,16,256]{2,1,0:T(8,128)(2,1)S(1)} async-done(((bf16[32,16,256]{2,1,0:T(8,128)(2,1)}), bf16[32,16,256]{2,1,0:T(8,128)(2,1)S(1)}, u32[]{:S(2)}, u32[]{:S(2)}) %all-to-all-start.1) | async-done | bytes 262176 | tf_op jit(solution)/shard_map/all_to_all | solution.py:443
  36.5 0.6 gather_fusion.4
  37.1 0.2 multiply_reduce_fusion
  37.3 0.7 copy.33
  38.0 0.7 broadcast_in_dim.64.square_ref
  38.7 67.3 %shard_map.100 = f32[32,8016]{1,0:T(8,128)} custom-call(bf16[16,4096]{1,0:T(8,128)(2,1)} %bitcast.93, f32[16,128]{1,0:T(8,128)} %broadcast_in_dim.64.square_ref, bf16[16,8016,256]{2,1,0:T(8,128)(2,1)} %bitcast.92), custom_call_target="tpu_custom_call" | custom-call | flops 8405385216 | bytes 65667072 | tf_op jit(solution)/shard_map/pallas_call | solution.py:348
  106.0 2.2 %copy.71 = f32[32,8016]{1,0:T(8,128)} copy(f32[32,8016]{1,0:T(8,128)} %shard_map.100) | data formatting | bytes 2052096
  (21 shorter events, 0.1 us)
Async XLA Ops:
  0.0 18.9 %copy-start = (bf16[16,128,256]{2,1,0:T(8,128)(2,1)S(1)}, bf16[16,128,256]{2,1,0:T(8,128)(2,1)}, u32[]{:S(2)}) copy-start(bf16[16,128,256]{2,1,0:T(8,128)(2,1)} %param.13) | copy-start | bytes 3145732
  0.0 18.1 %copy-start.2 = (s32[16]{0:T(128)S(1)}, s32[16]{0:T(128)}, u32[]{:S(2)}) copy-start(s32[16]{0:T(128)} %param.15) | copy-start | bytes 196
  19.8 3.1 %copy-start.3 = (bf16[16,128,256]{2,1,0:T(8,128)(2,1)S(1)}, bf16[16,128,256]{2,1,0:T(8,128)(2,1)}, u32[]{:S(2)}) copy-start(bf16[16,128,256]{2,1,0:T(8,128)(2,1)} %param.14) | copy-start | bytes 3145732
  21.1 1.2 %copy-start.4 = (f32[32,16,2,128]{3,1,2,0:T(8,128)}, f32[32,16,2,128]{3,1,2,0:T(8,128)S(1)}, u32[]{:S(2)}) copy-start(f32[32,16,2,128]{3,1,2,0:T(8,128)S(1)} %get-tuple-element.14) | copy-start | bytes 1572868
  21.1 1.1 %copy-start.6 = (f32[32,16,2]{1,2,0:T(2,128)}, f32[32,16,2]{1,2,0:T(2,128)S(1)}, u32[]{:S(2)}) copy-start(f32[32,16,2]{1,2,0:T(2,128)S(1)} %bitcast_maximum_fusion) | copy-start | bytes 12292
  23.6 6.0 %copy-start.7 = (bf16[16,256]{1,0:T(8,128)(2,1)S(1)}, bf16[16,256]{1,0:T(8,128)(2,1)}, u32[]{:S(2)}) copy-start(bf16[16,256]{1,0:T(8,128)(2,1)} %param.18) | copy-start | bytes 24580
  23.6 13.4 %copy-start.5 = (bf16[16,16,256]{2,1,0:T(8,128)(2,1)S(1)}, bf16[16,16,256]{2,1,0:T(8,128)(2,1)}, u32[]{:S(2)}) copy-start(bf16[16,16,256]{2,1,0:T(8,128)(2,1)} %param.17) | copy-start | bytes 393220
  26.2 10.3 %all-to-all-start.1 = ((bf16[32,16,256]{2,1,0:T(8,128)(2,1)}), bf16[32,16,256]{2,1,0:T(8,128)(2,1)S(1)}, u32[]{:S(2)}, u32[]{:S(2)}) async-start(bf16[32,16,256]{2,1,0:T(8,128)(2,1)} %bitcast.91), calls=%async_computation.1 | async-start | bytes 524288 | tf_op jit(solution)/shard_map/all_to_all | solution.py:443
  38.7 69.6 %copy-start.1 = (bf16[16,128,256]{2,1,0:T(8,128)(2,1)S(1)}, bf16[16,128,256]{2,1,0:T(8,128)(2,1)}, u32[]{:S(2)}) copy-start(bf16[16,128,256]{2,1,0:T(8,128)(2,1)} %param.13) | copy-start | bytes 3145732

commit v3 on v2

--- a/solution.py
+++ b/solution.py
@@ -69,6 +69,55 @@
     own_part = rounded_own[..., None] * fresh_value
     result = (summed + own_part) / weight_sum[..., None]
     return result.reshape(leading + (group_size, panel_width)).astype(jnp.bfloat16)
+
+
+def exchange_kernel(n_row, send_ref, out_ref, landing, send_sem, recv_sem):
+    row, col = lax.axis_index("row"), lax.axis_index("col")
+    barrier = pltpu.get_barrier_semaphore()
+    for k in range(1, n_row):
+        pl.semaphore_signal(
+            barrier, inc=1, device_id=(lax.rem(row + k, n_row), col), device_id_type=MESH
+        )
+    pl.semaphore_wait(barrier, n_row - 1)
+    copies = []
+    for k in range(1, n_row):
+        to_row = lax.rem(row + k, n_row)
+        copy = pltpu.make_async_remote_copy(
+            src_ref=send_ref.at[to_row],
+            dst_ref=landing.at[row],
+            send_sem=send_sem.at[k - 1],
+            recv_sem=recv_sem.at[k - 1],
+            device_id=(to_row, col),
+            device_id_type=MESH,
+        )
+        copy.start()
+        copies.append(copy)
+    landing[row] = send_ref[row]
+    for copy in copies:
+        copy.wait_recv()
+    out_ref[...] = landing[...]
+    for copy in copies:
+        copy.wait_send()
+
+
+def exchange(value, collective_id):
+    n_row, count, width = value.shape
+    if width % LANES or count % 16:
+        return lax.all_to_all(value, "row", split_axis=0, concat_axis=0, tiled=True)
+    vmem = pl.BlockSpec(memory_space=pltpu.VMEM)
+    return pl.pallas_call(
+        functools.partial(exchange_kernel, n_row),
+        out_shape=jax.ShapeDtypeStruct(value.shape, value.dtype),
+        in_specs=[vmem],
+        out_specs=vmem,
+        scratch_shapes=[
+            pltpu.VMEM(value.shape, value.dtype),
+            pltpu.SemaphoreType.DMA((n_row - 1,)),
+            pltpu.SemaphoreType.DMA((n_row - 1,)),
+        ],
+        compiler_params=pltpu.CompilerParams(collective_id=collective_id, has_side_effects=True),
+        cost_estimate=pl.CostEstimate(flops=0, bytes_accessed=4 * value.size, transcendentals=0),
+    )(value)
 
 
 def project_kernel(
@@ -426,21 +475,30 @@
     taken = slot_index[None, :] == jnp.arange(slots, dtype=jnp.int32)[:, None]
     child_of = jnp.sum(jnp.where(taken, jnp.arange(beam_count, dtype=jnp.int32)[None], 0), axis=1)
     offset = (parents % beam_count).astype(jnp.bfloat16)
-    offset_row = jnp.broadcast_to(offset[:, None, None], (beam_count, 1, panel_width))
+    offset_row = jnp.broadcast_to(offset[:, None], (beam_count, panel_width))
+    small = jnp.stack([new_keys, new_values, offset_row, offset_row], axis=1)
+    split = slot_cap * group_size
     request = jnp.concatenate(
-        [queries, new_keys[:, None], new_values[:, None], offset_row], axis=1
-    )[child_of]
-    asked = lax.all_to_all(request, "row", split_axis=0, concat_axis=0, tiled=True)
-    wanted = asked[:, group_size + 2, 0].astype(jnp.int32)
+        [
+            queries[child_of].reshape(row_count, split, panel_width),
+            small[child_of].reshape(row_count, 4 * slot_cap, panel_width),
+        ],
+        axis=1,
+    )
+    asked = exchange(request, 1)
+    asked_queries = asked[:, :split].reshape(slots, group_size, panel_width)
+    asked_small = asked[:, split:].reshape(slots, 4, panel_width)
+    wanted = asked_small[:, 2, 0].astype(jnp.int32)
     answer = attend(
-        asked[:, :group_size],
+        asked_queries,
         cache_keys[wanted],
         cache_values[wanted],
-        asked[:, group_size],
-        asked[:, group_size + 1],
+        asked_small[:, 0],
+        asked_small[:, 1],
         lengths[wanted],
     )
-    attended = lax.all_to_all(answer, "row", split_axis=0, concat_axis=0, tiled=True)[slot_index]
+    returned = exchange(answer.reshape(row_count, split, panel_width), 2)
+    attended = returned.reshape(slots, group_size, panel_width)[slot_index]
     stream = residual.astype(jnp.float32) + attended.astype(jnp.float32)
     if panel_width % LANES or vocab_weight.shape[2] % 16:
         return project_whole(stream, norm_gain, vocab_weight)

time: 109 us -> 109 us (level)
  Pallas kernels: 67.3 us -> 87.3 us
  blocking collectives: 13.3 us -> 0 us
  waiting for transfers between devices: 6.83 us -> 0 us
  local copies, waits for them, and re-layouts: 9.08 us -> 13.9 us
  starting transfers between devices: 3.41 us -> 0 us
  other arithmetic: 4.75 us -> 2.76 us
    pallas_call x0 -> x2, Pallas kernels: none -> 18.5 us  [exchange(): pl.pallas_call(functools.partial(exchange_kernel, n_row), out_shape=jax.S...]
    all_to_all x1 -> x0, blocking collectives: 13.3 us -> none  [body(): lax.all_to_all(request, 'row', split_axis=0, concat_axis=0, tiled=True)]
    all_to_all x1 -> x0, waiting for transfers between devices: 6.83 us -> none  [body(): lax.all_to_all(answer, 'row', split_axis=0, concat_axis=0, tiled=True)]
    all_to_all x1 -> x0, starting transfers between devices: 3.41 us -> none  [body(): lax.all_to_all(answer, 'row', split_axis=0, concat_axis=0, tiled=True)]
    gather x2 -> x3, local copies, waits for them, and re-layouts: 1.13 us -> 3.61 us  [the longest x1 1.51 us: body(): attended = returned.reshape(slots, group_size, panel_width)[slot_index]]
    another operation x0 -> x4, local copies, waits for them, and re-layouts: none -> 2.26 us  [the longest x3 1.51 us: body(): small = jnp.stack([new_keys, new_values, offset_row, offset_row], axis=1)]
    broadcast_in_dim x3 -> x0, local copies, waits for them, and re-layouts: 1.5 us -> none  [the longest x1 0.71 us: body(): new_keys[:, None]]
    pallas_call x1, Pallas kernels: 67.3 us -> 68.7 us  [project(): pl.pallas_call(functools.partial(project_kernel, n_row, n_col), out_shape...]
  transfers between devices with their start and end apart: 1 -> 0, of which waited for: 1 -> 0; matrix products, arithmetic and copies ran while one was open for 0% -> 0% of each run, Pallas kernels for 0% -> 0%
where the time goes in v3:
time: 109 us
  Pallas kernels  87.3 us (80%)
  local copies, waits for them, and re-layouts  13.9 us (13%)
  matrix products  4.38 us (4%)
  other arithmetic  2.76 us (3%)
    pallas_call x1, Pallas kernels, project(): pl.pallas_call(functools.partial(project_kernel, n_row, n_col), out_shape...  68.7 us
    pallas_call x2, Pallas kernels, exchange(): pl.pallas_call(functools.partial(exchange_kernel, n_row), out_shape=jax.S...  18.5 us
    unnamed x19, local copies, waits for them, and re-layouts  3.07 us
    dot_general x1, matrix products, attend(): jnp.einsum('...jhe,...the->...jht', query_heads, key_heads, preferred_ele...  2.35 us

profile of v3, /device:TPU:0, one launch (start us, length us, event | category | flops | bytes accessed | tf_op | source)
XLA Modules:
  0.0 108.6 jit_solution(8625480440148939081)
XLA Ops:
  0.0 0.8 and_select_fusion.1
  0.8 0.2 convert_reduce_fusion
  1.0 0.1 select_reduce_fusion.1
  1.1 0.1 stack_broadcast_in_dim.2
  1.2 0.7 copy.31
  1.9 0.7 copy.32
  2.6 0.1 pad_maximum_fusion.1
  2.7 0.6 gather_fusion.1
  3.3 1.5 %gather_fusion = bf16[32,16,256]{2,1,0:T(8,128)(2,1)S(1)} fusion(bf16[16,16,256]{2,1,0:T(8,128)(2,1)} %param.10, s32[1024]{0:T(1024)S(1)} %pad_clamp_fusion.2), kind=kCustom, calls=%fused_computation | custom fusion | bytes 524416 | tf_op jit(solution)/shard_map/gather | solution.py:483
  4.8 0.7 pad_maximum_fusion.send_ref
  5.6 10.4 %shard_map.100 = bf16[8,80,256]{2,1,0:T(8,128)(2,1)} custom-call(bf16[8,80,256]{2,1,0:T(8,128)(2,1)} %pad_maximum_fusion.send_ref), custom_call_target="tpu_custom_call" | custom-call | bytes 655360 | tf_op jit(solution)/shard_map/pallas_call | solution.py:108
  15.9 0.9 slice.15
  16.8 0.1 copy.41
  17.0 0.7 gather_fusion.3
  17.7 0.7 gather_fusion.4
  18.4 0.3 slice-done
  18.6 0.8 reshape_reshape.3
  19.4 2.4 %select_reduce_fusion = (f32[32,16,2]{1,2,0:T(2,128)S(1)}, f32[32,16,2,128]{3,1,2,0:T(8,128)S(1)}) fusion(s32[32]{0:T(128)S(1)} %gather_fusion.3, bf16[32,16,2,128]{3,2,1,0:T(2,128)(2,1)} %reshape_reshape.3, bf16[32,128,256]{2,1,0:T(8,128)(2,1)S(1)} %gather_fusion.4), kind=kOutput, calls=%fused_computation.19 | convolution fusion | flops 34077696 | bytes 2887808 | tf_op jit(solution)/shard_map/...jhe,...the->...jht/dot_general | solution.py:44
  21.8 0.2 fusion.30
  22.1 0.5 fusion.24
  22.6 0.7 gather_fusion.2
  23.4 0.0 copy-start.7
  23.4 1.8 %fusion.21 = bf16[32,16,2,128]{3,1,2,0:T(8,128)(2,1)S(1)} fusion(f32[32,16,2,128]{3,1,2,0:T(8,128)} %copy-done.4, f32[32,16,2]{1,2,0:T(2,128)S(1)} %get-tuple-element.10, f32[32,2,128]{2,1,0:T(2,128)S(1)} %bitcast.80, f32[32,16,2]{1,2,0:T(2,128)S(1)} %convert_element_type.65, f32[32,16,2]{1,2,0:T(2,128)S(1)} %bitcast_maximum_fusion, ...), kind=kOutput, calls=%fused_computation.17 | convolution fusion | flops 34603008 | bytes 2928768 | tf_op jit(solution)/shard_map/...jht,...the->...jhe/dot_general | solution.py:66
  25.2 0.2 copy.38
  25.4 0.9 convert_element_type.69.send_ref
  26.3 8.2 %shard_map.101 = bf16[8,64,256]{2,1,0:T(8,128)(2,1)} custom-call(bf16[8,64,256]{2,1,0:T(8,128)(2,1)} %convert_element_type.69.send_ref), custom_call_target="tpu_custom_call" | custom-call | bytes 524288 | tf_op jit(solution)/shard_map/pallas_call | solution.py:108
  34.5 1.5 %gather_fusion.5 = bf16[16,16,256]{2,1,0:T(8,128)(2,1)S(1)} fusion(bf16[32,16,256]{2,1,0:T(8,128)(2,1)} %bitcast.75, s32[1024]{0:T(1024)S(1)} %pad_clamp_fusion), kind=kCustom, calls=%fused_computation.5 | custom fusion | bytes 262208 | tf_op jit(solution)/shard_map/gather | solution.py:501
  36.0 0.2 multiply_reduce_fusion
  36.2 0.7 copy.46
  36.9 0.7 broadcast_in_dim.29.square_ref
  37.6 68.7 %shard_map.102 = f32[32,8016]{1,0:T(8,128)} custom-call(bf16[16,4096]{1,0:T(8,128)(2,1)} %bitcast.76, f32[16,128]{1,0:T(8,128)} %broadcast_in_dim.29.square_ref, bf16[16,8016,256]{2,1,0:T(8,128)(2,1)} %bitcast.73), custom_call_target="tpu_custom_call" | custom-call | flops 8405385216 | bytes 65667072 | tf_op jit(solution)/shard_map/pallas_call | solution.py:397
  106.3 2.2 %copy.76 = f32[32,8016]{1,0:T(8,128)} copy(f32[32,8016]{1,0:T(8,128)} %shard_map.102) | data formatting | bytes 2052096
  (30 shorter events, 0.3 us)
Async XLA Ops:
  0.0 17.7 %copy-start = (bf16[16,128,256]{2,1,0:T(8,128)(2,1)S(1)}, bf16[16,128,256]{2,1,0:T(8,128)(2,1)}, u32[]{:S(2)}) copy-start(bf16[16,128,256]{2,1,0:T(8,128)(2,1)} %param.13) | copy-start | bytes 3145732
  0.0 17.0 %copy-start.2 = (s32[16]{0:T(128)S(1)}, s32[16]{0:T(128)}, u32[]{:S(2)}) copy-start(s32[16]{0:T(128)} %param.15) | copy-start | bytes 196
  17.7 1.0 slice-start
  19.4 2.4 %copy-start.5 = (bf16[32,16,2,128]{3,2,1,0:T(2,128)(2,1)S(1)}, bf16[32,16,2,128]{3,2,1,0:T(2,128)(2,1)}, u32[]{:S(2)}) copy-start(bf16[32,16,2,128]{3,2,1,0:T(2,128)(2,1)} %reshape_reshape.3) | copy-start | bytes 786436
  19.4 3.2 %copy-start.3 = (bf16[16,128,256]{2,1,0:T(8,128)(2,1)S(1)}, bf16[16,128,256]{2,1,0:T(8,128)(2,1)}, u32[]{:S(2)}) copy-start(bf16[16,128,256]{2,1,0:T(8,128)(2,1)} %param.14) | copy-start | bytes 3145732
  21.7 0.9 copy-start.4
  23.4 12.6 %copy-start.7 = (bf16[16,256]{1,0:T(8,128)(2,1)S(1)}, bf16[16,256]{1,0:T(8,128)(2,1)}, u32[]{:S(2)}) copy-start(bf16[16,256]{1,0:T(8,128)(2,1)} %param.18) | copy-start | bytes 24580
  23.4 12.6 %copy-start.6 = (bf16[16,16,256]{2,1,0:T(8,128)(2,1)S(1)}, bf16[16,16,256]{2,1,0:T(8,128)(2,1)}, u32[]{:S(2)}) copy-start(bf16[16,16,256]{2,1,0:T(8,128)(2,1)} %param.17) | copy-start | bytes 393220
  37.6 71.0 %copy-start.1 = (bf16[16,128,256]{2,1,0:T(8,128)(2,1)S(1)}, bf16[16,128,256]{2,1,0:T(8,128)(2,1)}, u32[]{:S(2)}) copy-start(bf16[16,128,256]{2,1,0:T(8,128)(2,1)} %param.13) | copy-start | bytes 3145732
